TPU v7x, 128 devices: a whole 4x4x4 slice. The times are simulated.
128 devices in a mesh: ia: 8 (over z_lo, x), ja: 16 (over z_hi, y, core).
Axes of the slice: x: 4, y: 4, z: 4 (z_hi: 2, z_lo: 2; z = z_hi * 2 + z_lo), core: 2. Of those that a mesh axis runs over, the one named last changes fastest.
Arguments:
- tensor: float32 [8, 8192, 8192], P(None, 'ia', 'ja'), may hold values from -6 to 6
- b_init: float32 [8192, 64], P('ja'), may hold values from -0.0625 to 0.0625
- c_init: float32 [8, 64], replicated, may hold values from -6 to 6
Outputs:
- factor_a: float32 [8192, 64], P(('ia', 'ja'))
- factor_b: float32 [8192, 64], P('ja')
- factor_c: float32 [8, 64], replicated
All inputs are finite; a program needn't handle non-finite values.
Results may differ from a plain program's by a relative error of at most 0.0003.
Values sent between devices are 32-bit elements; how exact they have to be, the bound alone decides.
A program may use at most 128 MiB of HBM per device.

v0:
```python
import jax
import jax.numpy as jnp
from jax import lax
from jax.sharding import PartitionSpec as P

SWEEPS = 4


HIGH = lax.Precision.HIGHEST


def gram_of(factor):
    return jnp.dot(factor.T, factor, precision=HIGH, preferred_element_type=jnp.float32)


def solve_rows(products, normal):
    lower = jnp.linalg.cholesky(normal)
    return jax.scipy.linalg.cho_solve((lower, True), products.T).T


def unit_columns(factor, raw):
    norms = jnp.sqrt(jnp.diagonal(raw) + 1e-06)
    return (factor / norms[None, :], raw / (norms[:, None] * norms[None, :]))


def column_norms(raw):
    return jnp.sqrt(jnp.diagonal(raw) + 1e-06)


def body(tensor, b_init, c_init):
    factor_b = b_init
    factor_c = c_init
    gram_b = lax.psum(gram_of(factor_b), "ja")
    gram_c = gram_of(factor_c)
    rows_a = tensor.shape[1] // lax.axis_size("ja")
    stored = jnp.einsum("kij,jr->kir", tensor, factor_b, precision=HIGH)
    owned_a = None
    for sweep in range(SWEEPS):
        left_c = factor_c
        kept = stored
        mode_one = lax.psum_scatter(
            jnp.einsum("kir,kr->ir", kept, left_c, precision=HIGH),
            "ja",
            scatter_dimension=0,
            tiled=True,
        )
        solved_a = solve_rows(mode_one, gram_b * gram_c)
        block_a = lax.all_gather(solved_a, "ja", axis=0, tiled=True)
        local_gram_a = gram_of(block_a)
        partial_value = jnp.einsum("kij,ir->kjr", tensor, block_a, precision=HIGH)
        local_two = jnp.einsum("kjr,kr->jr", partial_value, left_c, precision=HIGH)
        mode_two, raw_a = lax.psum((local_two, local_gram_a), "ia")
        mode_two = mode_two / column_norms(raw_a)[None, :]
        block_a, gram_a = unit_columns(block_a, raw_a)
        factor_b = solve_rows(mode_two, gram_a * gram_c)
        local_gram_b = gram_of(factor_b)
        raw = lax.psum(local_gram_b, "ja")
        factor_b, gram_b = unit_columns(factor_b, raw)
        owned_a = lax.dynamic_slice_in_dim(block_a, lax.axis_index("ja") * rows_a, rows_a, 0)
        partial_value = jnp.einsum("kij,jr->kir", tensor, factor_b, precision=HIGH)
        local_three = jnp.einsum("kir,ir->kr", partial_value, block_a, precision=HIGH)
        mode_three = lax.psum(local_three, ("ia", "ja"))
        stored = partial_value
        factor_c = solve_rows(mode_three, gram_a * gram_b)
        gram_c = gram_of(factor_c)
    return (owned_a, factor_b, factor_c)


def solution(mesh):
    in_specs = (P(None, "ia", "ja"), P("ja", None), P())
    out_specs = (P(("ia", "ja"), None), P("ja", None), P())
    return jax.shard_map(body, mesh=mesh, in_specs=in_specs, out_specs=out_specs, check_vma=False)
```

profile of v0, /device:TPU:1, one launch (start us, length us, event | category | flops | bytes accessed | tf_op | source)
XLA Modules:
  0.0 1643.1 jit_solution(1288336324017532416)
XLA Ops:
  8.1 20.0 %fusion.40 = f32[8,1024,64]{1,2,0:T(8,128)S(1)} fusion(f32[8,1024,512]{2,1,0:T(8,128)} %param.10, f32[512,64]{0,1:T(8,128)S(1)} %copy-done), kind=kOutput, calls=%fused_computation.65 | convolution fusion | flops 3221225472 | bytes 19005440 | tf_op jit(solution)/shard_map/kij,jr->kir/dot_general | solution.py:36
  28.1 3.1 fusion.2
  32.5 66.7 %psum.119 = f32[64,64]{0,1:T(8,128)S(1)} all-reduce(f32[64,64]{0,1:T(8,128)S(1)} %fusion.153), channel_id=1, replica_groups=mesh['ia'=8,'ja'=16] {'ja'}, use_global_device_ids=true, to_apply=%region_0.0 | all-reduce | flops 4096 | bytes 32768 | tf_op jit(solution)/shard_map/psum | solution.py:33
  99.5 5.8 cholesky.194
  106.7 4.9 custom-call.42
  113.0 26.3 %all_gather.12 = f32[1024,64]{1,0:T(8,128)S(1)} all-gather(f32[64,64]{1,0:T(8,128)S(1)} %copy.69), channel_id=1, replica_groups=mesh['ia'=8,'ja'=16] {'ja'}, dimensions={0}, use_global_device_ids=true | all-gather | bytes 278528 | tf_op jit(solution)/shard_map/all_gather | solution.py:48
  140.4 14.1 convolution_bitcast_fusion.7
  154.4 26.7 %psum.120 = f32[64,64]{0,1:T(8,128)S(1)} all-reduce(f32[64,64]{0,1:T(8,128)S(1)} %fusion.154), channel_id=1, replica_groups=mesh['ia'=8,'ja'=16] {'ia'}, use_global_device_ids=true, to_apply=%region_4.7 | all-reduce | flops 4096 | bytes 32768 | tf_op jit(solution)/shard_map/psum | solution.py:52
  182.1 5.8 cholesky.205
  189.3 4.9 custom-call.43
  197.0 70.5 %all-reduce.5.cloned.1.call-done = f32[512,64]{0,1:T(8,128)} async-done(((f32[512,64]{0,1:T(8,128)}), f32[512,64]{0,1:T(8,128)}) %all-reduce.5.cloned.1.call-update) | async-done | bytes 131088 | tf_op jit(solution)/shard_map/psum | solution.py:52
  269.2 64.5 %psum.122 = f32[64,64]{0,1:T(8,128)S(1)} all-reduce(f32[64,64]{0,1:T(8,128)S(1)} %fusion.155), channel_id=1, replica_groups=mesh['ia'=8,'ja'=16] {'ja'}, use_global_device_ids=true, to_apply=%region_6.10 | all-reduce | flops 4096 | bytes 32768 | tf_op jit(solution)/shard_map/psum | solution.py:57
  334.7 20.4 %convolution_bitcast_fusion.3 = f32[8,1024,64]{1,2,0:T(8,128)S(1)} fusion(f32[8,1024,512]{2,1,0:T(8,128)} %param.10, f32[64,512]{1,0:T(8,128)S(1)} %fusion.114, f32[64]{0:T(128)S(1)} %add_sqrt_fusion.6), kind=kOutput, calls=%fused_computation.27 | convolution fusion | flops 3221258240 | bytes 19005696 | tf_op jit(solution)/shard_map/kij,jr->kir/dot_general | solution.py:60
  355.2 5.8 cholesky.216
  362.4 4.9 custom-call.44
  367.3 5.4 fusion.14
  372.7 67.8 %psum.123 = f32[64,8]{1,0:T(8,128)S(1)} all-reduce(f32[64,8]{1,0:T(8,128)S(1)} %bitcast.351), channel_id=1, replica_groups=mesh['ia'=8,'ja'=16] {'ia','ja'}, use_global_device_ids=true, to_apply=%region_7.11 | all-reduce | flops 512 | bytes 4096 | tf_op jit(solution)/shard_map/psum | solution.py:62
  444.2 5.8 cholesky.227
  452.6 4.9 custom-call.45
  457.5 54.5 %reduce-scatter.15.cloned.1.call-done = f32[64,64]{1,0:T(8,128)} async-done(((f32[1024,64]{1,0:T(8,128)}), f32[64,64]{1,0:T(8,128)}) %reduce-scatter.15.cloned.1.call-update) | async-done | bytes 16400
  513.4 25.4 %all_gather.13 = f32[1024,64]{1,0:T(8,128)S(1)} all-gather(f32[64,64]{1,0:T(8,128)S(1)} %copy.78), channel_id=1, replica_groups=mesh['ia'=8,'ja'=16] {'ja'}, dimensions={0}, use_global_device_ids=true | all-gather | bytes 278528 | tf_op jit(solution)/shard_map/all_gather | solution.py:48
  539.8 14.1 convolution_bitcast_fusion.6
  553.9 26.6 %psum.124 = f32[64,64]{0,1:T(8,128)S(1)} all-reduce(f32[64,64]{0,1:T(8,128)S(1)} %fusion.156), channel_id=1, replica_groups=mesh['ia'=8,'ja'=16] {'ia'}, use_global_device_ids=true, to_apply=%region_9.14 | all-reduce | flops 4096 | bytes 32768 | tf_op jit(solution)/shard_map/psum | solution.py:52
  581.5 5.8 cholesky.238
  588.7 4.9 custom-call.46
  596.2 71.0 %all-reduce.7.cloned.1.call-done = f32[512,64]{0,1:T(8,128)} async-done(((f32[512,64]{0,1:T(8,128)}), f32[512,64]{0,1:T(8,128)}) %all-reduce.7.cloned.1.call-update) | async-done | bytes 131088 | tf_op jit(solution)/shard_map/psum | solution.py:52
  668.9 64.5 %psum.126 = f32[64,64]{0,1:T(8,128)S(1)} all-reduce(f32[64,64]{0,1:T(8,128)S(1)} %fusion.157), channel_id=1, replica_groups=mesh['ia'=8,'ja'=16] {'ja'}, use_global_device_ids=true, to_apply=%region_11.16 | all-reduce | flops 4096 | bytes 32768 | tf_op jit(solution)/shard_map/psum | solution.py:57
  734.4 20.4 %convolution_bitcast_fusion.2 = f32[8,1024,64]{1,2,0:T(8,128)S(1)} fusion(f32[8,1024,512]{2,1,0:T(8,128)} %param.10, f32[64,512]{1,0:T(8,128)S(1)} %fusion.100, f32[64]{0:T(128)S(1)} %add_sqrt_fusion.4), kind=kOutput, calls=%fused_computation.26 | convolution fusion | flops 3221258240 | bytes 19005696 | tf_op jit(solution)/shard_map/kij,jr->kir/dot_general | solution.py:60
  754.9 5.8 cholesky.249
  762.1 4.9 custom-call.47
  767.0 5.4 fusion.10
  772.4 67.8 %psum.127 = f32[64,8]{1,0:T(8,128)S(1)} all-reduce(f32[64,8]{1,0:T(8,128)S(1)} %bitcast.352), channel_id=1, replica_groups=mesh['ia'=8,'ja'=16] {'ia','ja'}, use_global_device_ids=true, to_apply=%region_12.17 | all-reduce | flops 512 | bytes 4096 | tf_op jit(solution)/shard_map/psum | solution.py:62
  840.9 2.9 fusion.8
  843.9 5.8 cholesky.260
  852.4 4.9 custom-call.48
  857.3 54.5 %reduce-scatter.17.cloned.1.call-done = f32[64,64]{1,0:T(8,128)} async-done(((f32[1024,64]{1,0:T(8,128)}), f32[64,64]{1,0:T(8,128)}) %reduce-scatter.17.cloned.1.call-update) | async-done | bytes 16400
  913.1 25.4 %all_gather.14 = f32[1024,64]{1,0:T(8,128)S(1)} all-gather(f32[64,64]{1,0:T(8,128)S(1)} %copy.87), channel_id=1, replica_groups=mesh['ia'=8,'ja'=16] {'ja'}, dimensions={0}, use_global_device_ids=true | all-gather | bytes 278528 | tf_op jit(solution)/shard_map/all_gather | solution.py:48
  939.6 14.1 convolution_bitcast_fusion.5
  953.6 26.6 %psum.128 = f32[64,64]{0,1:T(8,128)S(1)} all-reduce(f32[64,64]{0,1:T(8,128)S(1)} %fusion.158), channel_id=1, replica_groups=mesh['ia'=8,'ja'=16] {'ia'}, use_global_device_ids=true, to_apply=%region_14.19 | all-reduce | flops 4096 | bytes 32768 | tf_op jit(solution)/shard_map/psum | solution.py:52
  981.3 5.8 cholesky.271
  988.5 4.9 custom-call.49
  995.9 71.0 %all-reduce.9.cloned.1.call-done = f32[512,64]{0,1:T(8,128)} async-done(((f32[512,64]{0,1:T(8,128)}), f32[512,64]{0,1:T(8,128)}) %all-reduce.9.cloned.1.call-update) | async-done | bytes 131088 | tf_op jit(solution)/shard_map/psum | solution.py:52
  1068.7 64.5 %psum.130 = f32[64,64]{0,1:T(8,128)S(1)} all-reduce(f32[64,64]{0,1:T(8,128)S(1)} %fusion.159), channel_id=1, replica_groups=mesh['ia'=8,'ja'=16] {'ja'}, use_global_device_ids=true, to_apply=%region_16.21 | all-reduce | flops 4096 | bytes 32768 | tf_op jit(solution)/shard_map/psum | solution.py:57
  1134.1 20.4 %convolution_bitcast_fusion.1 = f32[8,1024,64]{1,2,0:T(8,128)S(1)} fusion(f32[8,1024,512]{2,1,0:T(8,128)} %param.10, f32[64,512]{1,0:T(8,128)S(1)} %fusion.86, f32[64]{0:T(128)S(1)} %add_sqrt_fusion.2), kind=kOutput, calls=%fused_computation.25 | convolution fusion | flops 3221258240 | bytes 19005696 | tf_op jit(solution)/shard_map/kij,jr->kir/dot_general | solution.py:60
  1154.7 5.8 cholesky.282
  1161.8 4.9 custom-call.50
  1166.7 5.4 fusion.6
  1172.1 67.8 %psum.131 = f32[64,8]{1,0:T(8,128)S(1)} all-reduce(f32[64,8]{1,0:T(8,128)S(1)} %bitcast.353), channel_id=1, replica_groups=mesh['ia'=8,'ja'=16] {'ia','ja'}, use_global_device_ids=true, to_apply=%region_17.22 | all-reduce | flops 512 | bytes 4096 | tf_op jit(solution)/shard_map/psum | solution.py:62
  1240.7 2.9 fusion.4
  1243.6 5.8 cholesky.293
  1252.1 4.9 custom-call.51
  1257.0 54.5 %reduce-scatter.19.cloned.1.call-done = f32[64,64]{1,0:T(8,128)} async-done(((f32[1024,64]{1,0:T(8,128)}), f32[64,64]{1,0:T(8,128)}) %reduce-scatter.19.cloned.1.call-update) | async-done | bytes 16400
  1312.8 25.4 %all_gather.15 = f32[1024,64]{1,0:T(8,128)S(1)} all-gather(f32[64,64]{1,0:T(8,128)S(1)} %copy.96), channel_id=1, replica_groups=mesh['ia'=8,'ja'=16] {'ja'}, dimensions={0}, use_global_device_ids=true | all-gather | bytes 278528 | tf_op jit(solution)/shard_map/all_gather | solution.py:48
  1339.3 26.6 %psum.132 = f32[64,64]{0,1:T(8,128)S(1)} all-reduce(f32[64,64]{0,1:T(8,128)S(1)} %fusion.160), channel_id=1, replica_groups=mesh['ia'=8,'ja'=16] {'ia'}, use_global_device_ids=true, to_apply=%region_19.24 | all-reduce | flops 4096 | bytes 32768 | tf_op jit(solution)/shard_map/psum | solution.py:52
  1366.8 14.1 convolution_bitcast_fusion.4
  1381.1 5.8 cholesky.304
  1390.5 4.9 custom-call.52
  1396.2 65.0 %all-reduce.11.cloned.1.call-done = f32[512,64]{0,1:T(8,128)} async-done(((f32[512,64]{0,1:T(8,128)}), f32[512,64]{0,1:T(8,128)}) %all-reduce.11.cloned.1.call-update) | async-done | bytes 131088 | tf_op jit(solution)/shard_map/psum | solution.py:52
  1463.0 64.7 %psum.134 = f32[64,64]{0,1:T(8,128)S(1)} all-reduce(f32[64,64]{0,1:T(8,128)S(1)} %fusion.161), channel_id=1, replica_groups=mesh['ia'=8,'ja'=16] {'ja'}, use_global_device_ids=true, to_apply=%region_21.26 | all-reduce | flops 4096 | bytes 32768 | tf_op jit(solution)/shard_map/psum | solution.py:57
  1529.4 20.2 %convolution_bitcast_fusion = f32[8,1024,64]{1,2,0:T(8,128)S(1)} fusion(f32[8,1024,512]{2,1,0:T(8,128)} %param.10, f32[64,512]{1,0:T(8,128)S(1)} %fusion.72, f32[64]{0:T(128)S(1)} %add_sqrt_fusion), kind=kOutput, calls=%fused_computation.24 | convolution fusion | flops 3221258240 | bytes 19005696 | tf_op jit(solution)/shard_map/kij,jr->kir/dot_general | solution.py:60
  1549.8 5.8 cholesky.315
  1557.0 4.9 custom-call.53
  1561.9 5.4 fusion
  1567.2 67.8 %psum.135 = f32[64,8]{1,0:T(8,128)S(1)} all-reduce(f32[64,8]{1,0:T(8,128)S(1)} %bitcast.350), channel_id=1, replica_groups=mesh['ia'=8,'ja'=16] {'ia','ja'}, use_global_device_ids=true, to_apply=%region_22.27 | all-reduce | flops 512 | bytes 4096 | tf_op jit(solution)/shard_map/psum | solution.py:62
  (179 shorter events, 64.5 us)
Async XLA Ops:
  7.2 0.9 copy-start
  7.2 104.5 %reduce-scatter.13.cloned.1.call-start = ((), (), s32[]{:S(2)}) async-start(), calls=%async_computation.8 | async-start | bytes 557056
  28.1 71.1 %copy-start.1 = (f32[8,64]{1,0:T(8,128)S(1)}, f32[8,64]{1,0:T(8,128)}, u32[]{:S(2)}) copy-start(f32[8,64]{1,0:T(8,128)} %param.12) | copy-start | bytes 6148
  32.2 235.2 %all-reduce.5.cloned.1.call-start = ((), (), s32[]{:S(2)}) async-start(), calls=%async_computation.4 | async-start | bytes 262144 | tf_op jit(solution)/shard_map/psum | solution.py:52
  196.5 315.6 %reduce-scatter.15.cloned.1.call-start = ((), (), s32[]{:S(2)}) async-start(), calls=%async_computation.9 | async-start | bytes 557056
  451.1 216.1 %all-reduce.7.cloned.1.call-start = ((), (), s32[]{:S(2)}) async-start(), calls=%async_computation.5 | async-start | bytes 262144 | tf_op jit(solution)/shard_map/psum | solution.py:52
  595.9 315.9 %reduce-scatter.17.cloned.1.call-start = ((), (), s32[]{:S(2)}) async-start(), calls=%async_computation.10 | async-start | bytes 557056
  850.8 216.1 %all-reduce.9.cloned.1.call-start = ((), (), s32[]{:S(2)}) async-start(), calls=%async_computation.6 | async-start | bytes 262144 | tf_op jit(solution)/shard_map/psum | solution.py:52
  995.6 315.9 %reduce-scatter.19.cloned.1.call-start = ((), (), s32[]{:S(2)}) async-start(), calls=%async_computation.11 | async-start | bytes 557056
  1250.5 210.7 %all-reduce.11.cloned.1.call-start = ((), (), s32[]{:S(2)}) async-start(), calls=%async_computation.7 | async-start | bytes 262144 | tf_op jit(solution)/shard_map/psum | solution.py:52
Sparse Core Ops, SparseCore 0:
  32.3 66.8 reduce-scatter.12
  196.6 70.7 all-reduce.4
  451.2 60.8 reduce-scatter.14
  596.0 71.1 all-reduce.6
  850.9 60.8 reduce-scatter.16
  995.7 71.1 all-reduce.8
  1250.7 60.7 reduce-scatter.18
  1389.9 71.2 all-reduce.10
where the time goes:
time: 1650 us; the launch traced here: 1640 us
  blocking collectives  805 us (49%)
  waiting for transfers between devices  441 us (27%)
  matrix products  213 us (13%)
  other arithmetic  147 us (9%)
  local copies, waits for them, and re-layouts  20.2 us (1%)
    psum x4, waiting for transfers between devices, body(): mode_two, raw_a = lax.psum((local_two, local_gram_a), 'ia')  277 us
    psum x4, blocking collectives, body(): mode_three = lax.psum(local_three, ('ia', 'ja'))  271 us
    psum x4, blocking collectives, body(): raw = lax.psum(local_gram_b, 'ja')  258 us
    unnamed x12, waiting for transfers between devices  164 us
    psum x4, blocking collectives, body(): mode_two, raw_a = lax.psum((local_two, local_gram_a), 'ia')  107 us
    all_gather x4, blocking collectives, body(): block_a = lax.all_gather(solved_a, 'ja', axis=0, tiled=True)  103 us
    dot_general x4, matrix products, body(): partial_value = jnp.einsum('kij,jr->kir', tensor, factor_b, precision=HIGH)  81.5 us
    another operation x36, other arithmetic, solve_rows(): lower = jnp.linalg.cholesky(normal)  78.2 us
  transfers between devices with their start and end apart: 8, of which 7 were waited for; matrix products, arithmetic and copies ran while one was open for 2% of the time, Pallas kernels for 0%

commit v1 on v0

v1 whole, which is shorter than its diff:
```python
import functools

import jax
import jax.numpy as jnp
from jax import lax
from jax.experimental import pallas as pl
from jax.experimental.pallas import tpu as pltpu
from jax.sharding import PartitionSpec as P

SWEEPS = 4
K = 8
R = 64
NI = 8
NJ = 16
ROWS = 1024
COLS = 512
HIGH = lax.Precision.HIGHEST
F32 = jnp.float32
BF16 = jnp.bfloat16
MESH = pl.DeviceIdType.MESH


def dot(a, b, ca, cb, precision=None):
    return lax.dot_general(
        a, b, (((ca,), (cb,)), ((), ())), precision=precision, preferred_element_type=F32
    )


def split(x):
    high = x.astype(BF16)
    return high, (x - high.astype(F32)).astype(BF16)


def inverse(a, b=8):
    m = 8
    lane = lax.broadcasted_iota(jnp.int32, (m, R), 1)
    sub = lax.broadcasted_iota(jnp.int32, (m, R), 0)
    t = [a[8 * i : 8 * i + 8] for i in range(8)]

    def rep(v):
        return jnp.broadcast_to(v, (m, R))

    for k0 in range(0, R, b):
        kt, ks = k0 // 8, k0 % 8
        cols = [[rep(t[i][:, k0 + j : k0 + j + 1]) for i in range(8)] for j in range(b)]
        rows = [rep(t[kt][ks + j : ks + j + 1, :]) for j in range(b)]
        piv = [[rep(cols[j][kt][ks + i : ks + i + 1, :]) for j in range(b)] for i in range(b)]
        inside = (lane >= k0) & (lane < k0 + b)
        rows = [jnp.where(inside, jnp.where(lane == k0 + i, 1.0, 0.0), rows[i]) for i in range(b)]
        for i in range(b):
            p = 1.0 / piv[i][i]
            rows[i] = rows[i] * p
            for j in range(i + 1, b):
                piv[i][j] = piv[i][j] * p
            for r in range(b):
                if r != i:
                    f = piv[r][i]
                    for j in range(i + 1, b):
                        piv[r][j] = piv[r][j] - f * piv[i][j]
                    rows[r] = rows[r] - f * rows[i]
        for i in range(8):
            x = jnp.where(inside, 0.0, t[i])
            for j in range(b):
                x = x - cols[j][i] * rows[j]
            t[i] = x
        for j in range(b):
            t[kt] = jnp.where(sub == ks + j, rows[j], t[kt])
    return jnp.concatenate(t, axis=0)


def pack(gram):
    wide = jnp.concatenate([gram, jnp.zeros((R, 128 - R), F32)], axis=1)
    return wide[:32] + pltpu.roll(wide[32:], 64, 1)


def unpack(x):
    return jnp.concatenate([x[:, :R], pltpu.roll(x, 64, 1)[:, :R]], axis=0)


def diagonal(gram):
    same = lax.broadcasted_iota(jnp.int32, (R, R), 0) == lax.broadcasted_iota(jnp.int32, (R, R), 1)
    only = jnp.where(same, gram, 0.0)
    return jnp.sum(only, axis=0, keepdims=True), jnp.sum(only, axis=1, keepdims=True)


def unit(raw):
    row, col = diagonal(raw)
    row, col = jnp.sqrt(row + 1e-6), jnp.sqrt(col + 1e-6)
    return raw / (col * row), 1.0 / row, 1.0 / col


def turned(x):
    return jnp.concatenate([x, jnp.zeros_like(x)], axis=0).T


class Exchange:
    def __init__(self, axis, n, source, target, send, recv):
        me = lax.axis_index(axis)
        self.copies = []
        for d in range(1, n):
            peer = lax.rem(me + d, n)
            self.copies.append(
                pltpu.make_async_remote_copy(
                    src_ref=source(peer),
                    dst_ref=target(d),
                    send_sem=send.at[d],
                    recv_sem=recv.at[d],
                    device_id={axis: peer},
                    device_id_type=MESH,
                )
            )

    def start(self):
        for copy in self.copies:
            copy.start()

    def wait_recv(self):
        for copy in self.copies:
            copy.wait_recv()

    def wait_send(self):
        for copy in self.copies:
            copy.wait_send()


def kernel(
    t_hbm, b0, c0, out_a, out_b, out_c,
    stage, t16, prod, q_ref, w1, w2, at, bt, crow, ccol, gram_b, gram_c, scale_a, tmp,
    s1, r1, g1, s2, r2, g2, ga, gb, m3a, m3b,
    load_sem, s1s, s1r, g1s, g1r, s2s, s2r, g2s, g2r, gas, gar, gbs, gbr, mas, mar, mbs, mbr,
):
    me_i, me_j = lax.axis_index("ia"), lax.axis_index("ja")

    def load(k, slot):
        return pltpu.make_async_copy(t_hbm.at[k], stage.at[slot], load_sem.at[slot])

    load(0, 0).start()
    load(1, 1).start()

    barrier = pltpu.get_barrier_semaphore()
    for d in range(1, NJ):
        pl.semaphore_signal(barrier, inc=1, device_id={"ja": lax.rem(me_j + d, NJ)}, device_id_type=MESH)
    for d in range(1, NI):
        pl.semaphore_signal(barrier, inc=1, device_id={"ia": lax.rem(me_i + d, NI)}, device_id_type=MESH)
    pl.semaphore_wait(barrier, NJ - 1 + NI - 1)

    scatter1 = Exchange("ja", NJ, lambda p: s1.at[p], lambda d: r1.at[d], s1s, s1r)
    gather1 = Exchange("ja", NJ, lambda p: g1.at[me_j], lambda d: g1.at[me_j], g1s, g1r)
    scatter2 = Exchange("ia", NI, lambda p: s2.at[p], lambda d: r2.at[d], s2s, s2r)
    gather2 = Exchange("ia", NI, lambda p: g2.at[me_i], lambda d: g2.at[me_i], g2s, g2r)
    share_ga = Exchange("ia", NI, lambda p: ga.at[me_i], lambda d: ga.at[me_i], gas, gar)
    share_gb = Exchange("ja", NJ, lambda p: gb.at[me_j], lambda d: gb.at[me_j], gbs, gbr)
    share_ma = Exchange("ia", NI, lambda p: m3a.at[me_i], lambda d: m3a.at[me_i], mas, mar)
    share_mb = Exchange("ja", NJ, lambda p: m3b.at[me_j], lambda d: m3b.at[me_j], mbs, mbr)

    def total(ref, n):
        x = ref[0]
        for i in range(1, n):
            x = x + ref[i]
        return x

    def set_w1(b_t):
        high = b_t.astype(BF16).astype(F32)
        both = jnp.concatenate([high, b_t - high], axis=0).T
        w1[:COLS] = both.astype(BF16)
        keep = lax.broadcasted_iota(jnp.int32, (COLS, 128), 1) < R
        w1[COLS:] = jnp.where(keep, both, 0.0).astype(BF16)

    def products_b(k, _):
        prod[k] = dot(t16[k], w1[...], 1, 0)
        return 0

    def set_c(c, inv_norm):
        scaled = c * inv_norm
        crow[...] = jnp.concatenate([scaled, scaled], axis=1)
        wide = jnp.concatenate([c, jnp.zeros((K, 128 - R), F32)], axis=1)
        c_t = jnp.concatenate([wide, jnp.zeros((128 - K, 128), F32)], axis=0).T[:R]
        for k in range(K):
            ccol[k] = jnp.broadcast_to(c_t[:, k : k + 1], (R, 128))
        gram_c[...] = dot(c_t, c_t, 1, 1, HIGH)

    b_t = jnp.concatenate([b0[...], jnp.zeros((COLS, 128 - R), F32)], axis=1).T[:R]
    gb[me_j] = pack(dot(b_t, b_t, 1, 1, HIGH))
    share_gb.start()
    set_w1(b_t)
    set_c(c0[...], jnp.ones((1, R), F32))

    def first(k, _):
        slot = lax.rem(k, 2)
        load(k, slot).wait()
        high, low = split(stage[slot])
        t16[k, :, :COLS] = high
        t16[k, :, COLS:] = low

        @pl.when(k + 2 < K)
        def _():
            load(k + 2, slot).start()

        return products_b(k, 0)

    lax.fori_loop(0, K, first, 0)
    share_gb.wait_recv()
    gram_b[...] = unpack(total(gb, NJ))
    share_gb.wait_send()

    def sweep(s, _):
        for q in range(8):
            rows = pl.ds(128 * q, 128)
            acc = prod[0, rows, :] * crow[0:1]
            for k in range(1, K):
                acc = acc + prod[k, rows, :] * crow[k : k + 1]
            acc = acc.T
            acc = acc[:R] + acc[R:]
            s1[2 * q] = acc[:32]
            s1[2 * q + 1] = acc[32:]
        scatter1.start()
        solve_a = inverse(gram_b[...] * gram_c[...])
        scatter1.wait_recv()
        acc = s1[me_j]
        for d in range(1, NJ):
            acc = acc + r1[d]
        g1[me_j] = acc
        gather1.start()
        gather1.wait_recv()
        for q in range(8):
            block = jnp.concatenate([g1[2 * q], g1[2 * q + 1]], axis=0)
            block = dot(solve_a, block, 1, 0, HIGH)
            at[q] = block
            high, low = split(block)
            w2[:R, 128 * q : 128 * q + 128] = high
            w2[R:, 128 * q : 128 * q + 128] = low
        a_t = jnp.concatenate([at[q] for q in range(8)], axis=1)
        ga[me_i] = pack(dot(a_t, a_t, 1, 1, HIGH))
        share_ga.start()

        def products_a(k, acc):
            x = dot(w2[...], t16[k], 1, 0)
            x = x[:R, :COLS] + x[R:, :COLS] + x[:R, COLS:]
            q_ref[k] = x
            c = ccol[k]
            return acc + x * jnp.concatenate([c] * 4, axis=1)

        acc = lax.fori_loop(0, K, products_a, jnp.zeros((R, COLS), F32))
        for j in range(4):
            s2[2 * j] = acc[:32, 128 * j : 128 * j + 128]
            s2[2 * j + 1] = acc[32:, 128 * j : 128 * j + 128]
        scatter2.start()
        share_ga.wait_recv()
        gram_a, row_a, col_a = unit(unpack(total(ga, NI)))
        scale_a[...] = jnp.broadcast_to(col_a, (R, 128))
        solve_b = inverse(gram_a * gram_c[...]) * row_a
        scatter2.wait_recv()
        acc = s2[me_i]
        for d in range(1, NI):
            acc = acc + r2[d]
        g2[me_i] = acc
        gather2.start()
        gather2.wait_recv()
        acc = jnp.concatenate(
            [jnp.concatenate([g2[2 * j], g2[2 * j + 1]], axis=0) for j in range(4)], axis=1
        )
        b_t = dot(solve_b, acc, 1, 0, HIGH)
        bt[...] = b_t

        scaled = b_t * col_a
        lane = lax.broadcasted_iota(jnp.int32, (R, 128), 1)
        sums = jnp.zeros((R, 128), F32)
        for k in range(K):
            x = q_ref[k] * scaled
            x = x[:, :128] + x[:, 128:256] + x[:, 256:384] + x[:, 384:]
            sums = jnp.where(lane == k, jnp.sum(x, axis=1, keepdims=True), sums)
        m3a[me_i] = turned(sums)[:K]
        share_ma.start()
        gb[me_j] = pack(dot(b_t, b_t, 1, 1, HIGH))
        share_gb.start()

        @pl.when(s < SWEEPS - 1)
        def _():
            set_w1(b_t)
            lax.fori_loop(0, K // 2, products_b, 0)

        share_ma.wait_recv()
        m3b[me_j] = total(m3a, NI)
        share_mb.start()

        @pl.when(s < SWEEPS - 1)
        def _():
            lax.fori_loop(K // 2, K, products_b, 0)

        share_gb.wait_recv()
        unit_b, row_b, col_b = unit(unpack(total(gb, NJ)))
        gram_b[...] = unit_b
        tmp[:R] = jnp.broadcast_to(col_b, (R, 128))
        solve_c = inverse(gram_a * unit_b)
        share_mb.wait_recv()
        c = dot(total(m3b, NJ)[:, :R] * row_b, solve_c, 1, 0, HIGH)
        out_c[...] = c
        set_c(c, row_b)
        for exchange in (scatter1, gather1, scatter2, gather2, share_ga, share_gb, share_ma, share_mb):
            exchange.wait_send()
        return 0

    lax.fori_loop(0, SWEEPS, sweep, 0)
    scale = tmp[:R]
    scale = jnp.concatenate([scale] * 4, axis=1)
    out_b[...] = turned(bt[...] * scale)[:, :R]
    tmp[...] = turned(at[me_j // 2] * scale_a[...])
    out_a[...] = tmp[pl.ds(pl.multiple_of(R * lax.rem(me_j, 2), R), R), :R]


def body(tensor, b_init, c_init):
    vmem = pl.BlockSpec(memory_space=pltpu.VMEM)

    def dma(n):
        return pltpu.SemaphoreType.DMA((n,))

    def slices(n):
        return pltpu.VMEM((n, 32, 128), F32)

    return pl.pallas_call(
        kernel,
        out_shape=(
            jax.ShapeDtypeStruct((R, R), F32),
            jax.ShapeDtypeStruct((COLS, R), F32),
            jax.ShapeDtypeStruct((K, R), F32),
        ),
        in_specs=[pl.BlockSpec(memory_space=pl.ANY), vmem, vmem],
        out_specs=(vmem, vmem, vmem),
        scratch_shapes=[
            pltpu.VMEM((2, ROWS, COLS), F32),
            pltpu.VMEM((K, ROWS, 2 * COLS), BF16),
            pltpu.VMEM((K, ROWS, 128), F32),
            pltpu.VMEM((K, R, COLS), F32),
            pltpu.VMEM((2 * COLS, 128), BF16),
            pltpu.VMEM((2 * R, ROWS), BF16),
            pltpu.VMEM((8, R, 128), F32),
            pltpu.VMEM((R, COLS), F32),
            pltpu.VMEM((K, 128), F32),
            pltpu.VMEM((K, R, 128), F32),
            pltpu.VMEM((R, R), F32),
            pltpu.VMEM((R, R), F32),
            pltpu.VMEM((R, 128), F32),
            pltpu.VMEM((128, 128), F32),
            slices(NJ), slices(NJ), slices(NJ),
            slices(NI), slices(NI), slices(NI),
            slices(NI), slices(NJ),
            pltpu.VMEM((NI, K, 128), F32),
            pltpu.VMEM((NJ, K, 128), F32),
            dma(2),
            dma(NJ), dma(NJ), dma(NJ), dma(NJ),
            dma(NI), dma(NI), dma(NI), dma(NI),
            dma(NI), dma(NI), dma(NJ), dma(NJ),
            dma(NI), dma(NI), dma(NJ), dma(NJ),
        ],
        compiler_params=pltpu.CompilerParams(
            collective_id=0, has_side_effects=True, vmem_limit_bytes=48 * 1024 * 1024
        ),
    )(tensor, b_init, c_init)


def solution(mesh):
    in_specs = (P(None, "ia", "ja"), P("ja", None), P())
    out_specs = (P(("ia", "ja"), None), P("ja", None), P())
    return jax.shard_map(body, mesh=mesh, in_specs=in_specs, out_specs=out_specs, check_vma=False)
```

time: 1650 us -> 167 us (0.10)
  blocking collectives: 805 us -> 0 us
  waiting for transfers between devices: 441 us -> 0 us
  matrix products: 213 us -> 0 us
  Pallas kernels: 0 us -> 163 us
  other arithmetic: 147 us -> 0 us
  local copies, waits for them, and re-layouts: 20.2 us -> 3.69 us
    psum x13 -> x0, blocking collectives: 703 us -> none  [the longest x4 271 us: body(): mode_three = lax.psum(local_three, ('ia', 'ja'))]
    psum x4 -> x0, waiting for transfers between devices: 277 us -> none  [body(): mode_two, raw_a = lax.psum((local_two, local_gram_a), 'ia')]
    dot_general x34 -> x0, matrix products: 204 us -> none  [the longest x4 81.5 us: body(): partial_value = jnp.einsum('kij,jr->kir', tensor, factor_b, precision=HIGH)]
    unnamed x12 -> x0, waiting for transfers between devices: 164 us -> none
    pallas_call x0 -> x1, Pallas kernels: none -> 163 us  [body(): pl.pallas_call(kernel, out_shape=(jax.ShapeDtypeStruct((R, R), F32), jax....]
    another operation x60 -> x0, other arithmetic: 145 us -> none  [the longest x36 78.2 us: solve_rows(): lower = jnp.linalg.cholesky(normal)]
    all_gather x4 -> x0, blocking collectives: 103 us -> none  [body(): block_a = lax.all_gather(solved_a, 'ja', axis=0, tiled=True)]
  transfers between devices with their start and end apart: 8 -> 0, of which waited for: 7 -> 0; matrix products, arithmetic and copies ran while one was open for 2% -> 0% of each run, Pallas kernels for 0% -> 0%
where the time goes in v1:
time: 167 us
  Pallas kernels  163 us (98%)
  local copies, waits for them, and re-layouts  3.69 us (2%)
    pallas_call x1, Pallas kernels, body(): pl.pallas_call(kernel, out_shape=(jax.ShapeDtypeStruct((R, R), F32), jax....  163 us

profile of v1, /device:TPU:1, one launch (start us, length us, event | category | flops | bytes accessed | tf_op | source)
XLA Modules:
  0.0 167.0 jit_solution(2126852291453718115)
XLA Ops:
  0.6 1.0 copy.6.b0
  1.7 0.0 copy-start
  1.7 0.7 copy-done
  2.4 162.6 %shard_map.58 = (f32[64,64]{1,0:T(8,128)S(1)}, f32[512,64]{1,0:T(8,128)S(1)}, f32[8,64]{1,0:T(8,128)S(1)}) custom-call(f32[8,1024,512]{2,1,0:T(8,128)} %t_hbm.1, f32[512,64]{1,0:T(8,128)S(1)} %copy.6.b0, f32[8,64]{1,0:T(8,128)S(1)} %copy-done), custom_call_target="tpu_custom_call" | custom-call | tf_op jit(solution)/shard_map/pallas_call | solution.py:320
  165.0 0.8 copy.7
  165.8 0.6 copy.10
  166.4 0.6 copy.11
Async XLA Ops:
  1.7 0.7 copy-start

commit v2 on v1

v2 whole, which is shorter than its diff:
```python
import functools

import jax
import jax.numpy as jnp
from jax import lax
from jax.experimental import pallas as pl
from jax.experimental.pallas import tpu as pltpu
from jax.sharding import PartitionSpec as P

SWEEPS = 4
K = 8
R = 64
NI = 8
NJ = 16
ROWS = 1024
COLS = 512
HIGH = lax.Precision.HIGHEST
F32 = jnp.float32
BF16 = jnp.bfloat16
MESH = pl.DeviceIdType.MESH


def dot(a, b, ca, cb, precision=None):
    return lax.dot_general(
        a, b, (((ca,), (cb,)), ((), ())), precision=precision, preferred_element_type=F32
    )


def split(x):
    high = x.astype(BF16)
    return high, (x - high.astype(F32)).astype(BF16)


def inverse(a):
    m = 8
    lane = lax.broadcasted_iota(jnp.int32, (m, R), 1)
    sub = lax.broadcasted_iota(jnp.int32, (m, R), 0)
    t = [a[m * i : m * i + m] for i in range(R // m)]

    def rep(v):
        return jnp.broadcast_to(v, (m, R))

    for k0 in range(0, R, m):
        kt = k0 // m
        inside = (lane >= k0) & (lane < k0 + m)
        cols = [[rep(x[:, k0 + j : k0 + j + 1]) for x in t] for j in range(m)]
        panel = jnp.where(inside, jnp.where(lane - k0 == sub, 1.0, 0.0), t[kt])
        block = [cols[j][kt] for j in range(m)]
        for i in range(m):
            p = 1.0 / rep(block[i][i : i + 1, :])
            row = rep(panel[i : i + 1, :]) * p
            f = jnp.where(sub == i, 0.0, block[i])
            panel = jnp.where(sub == i, row, panel) - f * row
            for j in range(i + 1, m):
                row = rep(block[j][i : i + 1, :]) * p
                block[j] = jnp.where(sub == i, row, block[j]) - f * row
        rows = [rep(panel[j : j + 1, :]) for j in range(m)]
        for i in range(R // m):
            if i == kt:
                continue
            even, odd = cols[0][i] * rows[0], cols[1][i] * rows[1]
            for j in range(2, m, 2):
                even, odd = even + cols[j][i] * rows[j], odd + cols[j + 1][i] * rows[j + 1]
            t[i] = jnp.where(inside, 0.0, t[i]) - (even + odd)
        t[kt] = panel
    return jnp.concatenate(t, axis=0)


def pack(gram):
    wide = jnp.concatenate([gram, jnp.zeros((R, 128 - R), F32)], axis=1)
    return wide[:32] + pltpu.roll(wide[32:], 64, 1)


def unpack(x):
    return jnp.concatenate([x[:, :R], pltpu.roll(x, 64, 1)[:, :R]], axis=0)


def diagonal(gram):
    same = lax.broadcasted_iota(jnp.int32, (R, R), 0) == lax.broadcasted_iota(jnp.int32, (R, R), 1)
    only = jnp.where(same, gram, 0.0)
    return jnp.sum(only, axis=0, keepdims=True), jnp.sum(only, axis=1, keepdims=True)


def unit(raw):
    row, col = diagonal(raw)
    row, col = jnp.sqrt(row + 1e-6), jnp.sqrt(col + 1e-6)
    return raw / (col * row), 1.0 / row, 1.0 / col


def turned(x):
    return jnp.concatenate([x, jnp.zeros_like(x)], axis=0).T


class Exchange:
    def __init__(self, axis, n, source, slots, send, recv):
        self.axis, self.n, self.source, self.slots, self.send, self.recv = axis, n, source, slots, send, recv
        self.me = lax.axis_index(axis)

    def copy(self, peer):
        return pltpu.make_async_remote_copy(
            src_ref=self.source(peer),
            dst_ref=self.slots.at[self.me],
            send_sem=self.send.at[peer],
            recv_sem=self.recv.at[self.me],
            device_id={self.axis: peer},
            device_id_type=MESH,
        )

    def start(self, peer):
        self.copy(peer).start()

    def start_all(self):
        for d in range(1, self.n):
            self.start(lax.rem(self.me + d, self.n))

    def wait_from(self, peer):
        pltpu.make_async_remote_copy(
            src_ref=self.source(peer),
            dst_ref=self.slots.at[peer],
            send_sem=self.send.at[peer],
            recv_sem=self.recv.at[peer],
            device_id={self.axis: peer},
            device_id_type=MESH,
        ).wait_recv()

    def wait_all(self):
        for d in range(1, self.n):
            self.wait_from(lax.rem(self.me + d, self.n))

    def wait_sent(self):
        for d in range(1, self.n):
            self.copy(lax.rem(self.me + d, self.n)).wait_send()


def kernel(
    t_hbm, b_hbm, c_hbm, out_a, out_b, out_c,
    b0, c_now, stage, t16, prod, q_ref, m2, w1, at, bt, crow, ccol, gram_b, gram_c, scale_a, scale_b, tmp,
    s1, r1, g1, s2, r2, g2, ga, gb, m3a, m3b,
    load_sem, small_sem, s1s, s1r, g1s, g1r, s2s, s2r, g2s, g2r, gas, gar, gbs, gbr, mas, mar, mbs, mbr,
):
    me_i, me_j = lax.axis_index("ia"), lax.axis_index("ja")
    me_q = me_j // 2
    partner = me_j + 1 - 2 * lax.rem(me_j, 2)

    def load(n):
        k, rows = n // 2, pl.ds(ROWS // 2 * (n % 2), ROWS // 2)
        return pltpu.make_async_copy(t_hbm.at[k, rows], stage.at[k, rows], load_sem.at[n])

    load_b = pltpu.make_async_copy(b_hbm, b0, small_sem.at[0])
    load_c = pltpu.make_async_copy(c_hbm, c_now, small_sem.at[1])
    load_b.start()
    load_c.start()
    for n in range(2 * K):
        load(n).start()

    barrier = pltpu.get_barrier_semaphore()
    for d in range(1, NJ):
        pl.semaphore_signal(barrier, inc=1, device_id={"ja": lax.rem(me_j + d, NJ)}, device_id_type=MESH)
    for d in range(1, NI):
        pl.semaphore_signal(barrier, inc=1, device_id={"ia": lax.rem(me_i + d, NI)}, device_id_type=MESH)

    scatter1 = Exchange("ja", NJ, lambda p: s1.at[p], r1, s1s, s1r)
    gather1 = Exchange("ja", NJ, lambda p: g1.at[me_j], g1, g1s, g1r)
    scatter2 = Exchange("ia", NI, lambda p: s2.at[p], r2, s2s, s2r)
    gather2 = Exchange("ia", NI, lambda p: g2.at[me_i], g2, g2s, g2r)
    share_ga = Exchange("ia", NI, lambda p: ga.at[me_i], ga, gas, gar)
    share_gb = Exchange("ja", NJ, lambda p: gb.at[me_j], gb, gbs, gbr)
    share_ma = Exchange("ia", NI, lambda p: m3a.at[me_i], m3a, mas, mar)
    share_mb = Exchange("ja", NJ, lambda p: m3b.at[me_j], m3b, mbs, mbr)

    def total(ref, n):
        x = ref[0]
        for i in range(1, n):
            x = x + ref[i]
        return x

    def set_w1(b_t):
        high = b_t.astype(BF16).astype(F32)
        both = jnp.concatenate([high, b_t - high], axis=0).T
        w1[:COLS] = both.astype(BF16)
        keep = lax.broadcasted_iota(jnp.int32, (COLS, 128), 1) < R
        w1[COLS:] = jnp.where(keep, both, 0.0).astype(BF16)

    def products_b(k):
        prod[k] = dot(t16[k], w1[...], 1, 0)

    def set_rows(c, inv_norm):
        scaled = c * inv_norm
        crow[...] = jnp.concatenate([scaled, scaled], axis=1)

    def set_c(c):
        wide = jnp.concatenate([c, jnp.zeros((K, 128 - R), F32)], axis=1)
        c_t = jnp.concatenate([wide, jnp.zeros((128 - K, 128), F32)], axis=0).T[:R]
        for k in range(K):
            ccol[k] = jnp.broadcast_to(c_t[:, k : k + 1], (R, 128))
        gram_c[...] = dot(c_t, c_t, 1, 1, HIGH)

    load_b.wait()
    load_c.wait()
    b_t = b0[...]
    set_w1(b_t)
    set_rows(c_now[...], jnp.ones((1, R), F32))
    gb[me_j] = pack(dot(b_t, b_t, 1, 1, HIGH))
    for n in range(2 * K):
        k, rows = n // 2, slice(ROWS // 2 * (n % 2), ROWS // 2 * (n % 2 + 1))
        load(n).wait()
        high, low = split(stage[k, rows])
        t16[k, rows, :COLS] = high
        t16[k, rows, COLS:] = low
        prod[k, rows] = dot(t16[k, rows], w1[...], 1, 0)
        if n == 10:
            pl.semaphore_wait(barrier, NJ - 1 + NI - 1)
            share_gb.start_all()

    def sweep(s, _):
        for e in (4, 5, 3, 6, 2, 7, 1, 0):
            q = lax.rem(me_q + e, 8)
            rows = pl.ds(pl.multiple_of(128 * q, 128), 128)
            acc = prod[0, rows, :] * crow[0:1]
            for k in range(1, K):
                acc = acc + prod[k, rows, :] * crow[k : k + 1]
            acc = acc.T
            acc = acc[:R] + acc[R:]
            s1[2 * q] = acc[:32]
            s1[2 * q + 1] = acc[32:]
            if e:
                scatter1.start(2 * q)
                scatter1.start(2 * q + 1)
            else:
                scatter1.start(partner)
        set_c(c_now[...])
        q_ref[...] = jnp.zeros_like(q_ref)
        m2[...] = jnp.zeros_like(m2)

        @pl.when(s == 0)
        def _():
            share_gb.wait_all()
            gram_b[...] = unpack(total(gb, NJ))
            share_gb.wait_sent()

        @pl.when(s > 0)
        def _():
            share_mb.wait_sent()

        solve_a = inverse(gram_b[...] * gram_c[...])
        scatter1.wait_from(partner)
        acc = s1[me_j] + r1[partner]
        for e in (1, 7, 4, 3, 5, 2, 6):
            for h in range(2):
                j = 2 * lax.rem(me_q + e, 8) + h
                scatter1.wait_from(j)
                acc = acc + r1[j]
        g1[me_j] = acc
        for e in (6, 2, 5, 3, 4, 7, 1):
            for h in range(2):
                gather1.start(2 * lax.rem(me_q + e, 8) + h)
        gather1.start(partner)
        scatter1.wait_sent()

        z, y = me_j // 8, lax.rem(me_j // 4, 2)

        def quarter(n, _):
            g = 2 * lax.rem(z + n // 2, 2) + lax.rem(y + n, 2)
            for e in range(4):

                @pl.when(4 * g + e != me_j)
                def _(e=e):
                    gather1.wait_from(4 * g + e)

            block = jnp.concatenate(
                [
                    jnp.concatenate([g1[4 * g], g1[4 * g + 1]], axis=0),
                    jnp.concatenate([g1[4 * g + 2], g1[4 * g + 3]], axis=0),
                ],
                axis=1,
            )
            block = dot(solve_a, block, 1, 0, HIGH)
            at[g] = block
            both = jnp.concatenate(split(block), axis=0)
            rows = pl.ds(pl.multiple_of(256 * g, 256), 256)
            acc = m2[...]
            for k in range(K):
                x = dot(both, t16[k, rows, :], 1, 0)
                x = x[:R, :COLS] + x[R:, :COLS] + x[:R, COLS:]
                q_ref[k] = q_ref[k] + x
                acc = acc + x * jnp.concatenate([ccol[k]] * 4, axis=1)
            m2[...] = acc
            return 0

        lax.fori_loop(0, 4, quarter, 0)
        for p in range(NI):
            j, h = p // 2, p % 2
            s2[p] = m2[32 * h : 32 * h + 32, 128 * j : 128 * j + 128]
        for d in (6, 2, 5, 3, 7, 1, 4):
            scatter2.start(lax.rem(me_i + d, NI))
        a_t = jnp.concatenate([at[g] for g in range(4)], axis=1)
        ga[me_i] = pack(dot(a_t, a_t, 1, 1, HIGH))
        share_ga.start_all()
        gather1.wait_sent()
        acc = s2[me_i]
        for d in (4, 1, 7, 3, 5, 2, 6):
            j = lax.rem(me_i + d, NI)
            scatter2.wait_from(j)
            acc = acc + r2[j]
        g2[me_i] = acc
        for d in (6, 2, 5, 3, 7, 1, 4):
            gather2.start(lax.rem(me_i + d, NI))
        share_ga.wait_all()
        scatter2.wait_sent()
        gram_a, row_a, col_a = unit(unpack(total(ga, NI)))
        scale_a[...] = jnp.broadcast_to(col_a, (R, 128))
        solve_b = inverse(gram_a * gram_c[...]) * row_a
        gather2.wait_all()
        acc = jnp.concatenate(
            [jnp.concatenate([g2[2 * j], g2[2 * j + 1]], axis=0) for j in range(4)], axis=1
        )
        b_t = dot(solve_b, acc, 1, 0, HIGH)
        bt[...] = b_t

        scaled = b_t * col_a
        lane = lax.broadcasted_iota(jnp.int32, (R, 128), 1)
        sums = jnp.zeros((R, 128), F32)
        for k in range(K):
            x = q_ref[k] * scaled
            x = x[:, :128] + x[:, 128:256] + x[:, 256:384] + x[:, 384:]
            sums = jnp.where(lane == k, jnp.sum(x, axis=1, keepdims=True), sums)
        m3a[me_i] = turned(sums)[:K]
        share_ma.start_all()
        gb[me_j] = pack(dot(b_t, b_t, 1, 1, HIGH))
        share_gb.start_all()

        @pl.when(s < SWEEPS - 1)
        def _():
            set_w1(b_t)
            for k in range(K // 2):
                products_b(k)

        share_ma.wait_all()
        m3b[me_j] = total(m3a, NI)
        share_mb.start_all()

        @pl.when(s < SWEEPS - 1)
        def _():
            for k in range(K // 2, K):
                products_b(k)

        for exchange in (gather2, share_ga, share_ma):
            exchange.wait_sent()
        share_gb.wait_all()
        unit_b, row_b, col_b = unit(unpack(total(gb, NJ)))
        gram_b[...] = unit_b
        scale_b[...] = jnp.broadcast_to(col_b, (R, 128))
        solve_c = inverse(gram_a * unit_b)
        share_gb.wait_sent()
        share_mb.wait_all()
        c = dot(total(m3b, NJ)[:, :R] * row_b, solve_c, 1, 0, HIGH)
        c_now[...] = c
        set_rows(c, row_b)
        return 0

    lax.fori_loop(0, SWEEPS, sweep, 0)
    share_mb.wait_sent()
    out_c[...] = c_now[...]
    out_b[...] = bt[...] * jnp.concatenate([scale_b[...]] * 4, axis=1)
    tmp[...] = turned(at[me_j // 4] * jnp.concatenate([scale_a[...]] * 2, axis=1))
    out_a[...] = tmp[pl.ds(pl.multiple_of(R * lax.rem(me_j, 4), R), R), :R]


def body(tensor, b_init, c_init):
    vmem = pl.BlockSpec(memory_space=pltpu.VMEM)

    def dma(n):
        return pltpu.SemaphoreType.DMA((n,))

    def slices(n):
        return pltpu.VMEM((n, 32, 128), F32)

    a, b, c = pl.pallas_call(
        kernel,
        out_shape=(
            jax.ShapeDtypeStruct((R, R), F32),
            jax.ShapeDtypeStruct((R, COLS), F32),
            jax.ShapeDtypeStruct((K, R), F32),
        ),
        in_specs=[pl.BlockSpec(memory_space=pltpu.HBM)] * 3,
        out_specs=(vmem, vmem, vmem),
        scratch_shapes=[
            pltpu.VMEM((R, COLS), F32),
            pltpu.VMEM((K, R), F32),
            pltpu.VMEM((K, ROWS, COLS), F32),
            pltpu.VMEM((K, ROWS, 2 * COLS), BF16),
            pltpu.VMEM((K, ROWS, 128), F32),
            pltpu.VMEM((K, R, COLS), F32),
            pltpu.VMEM((R, COLS), F32),
            pltpu.VMEM((2 * COLS, 128), BF16),
            pltpu.VMEM((4, R, 256), F32),
            pltpu.VMEM((R, COLS), F32),
            pltpu.VMEM((K, 128), F32),
            pltpu.VMEM((K, R, 128), F32),
            pltpu.VMEM((R, R), F32),
            pltpu.VMEM((R, R), F32),
            pltpu.VMEM((R, 128), F32),
            pltpu.VMEM((R, 128), F32),
            pltpu.VMEM((256, 128), F32),
            slices(NJ), slices(NJ), slices(NJ),
            slices(NI), slices(NI), slices(NI),
            slices(NI), slices(NJ),
            pltpu.VMEM((NI, K, 128), F32),
            pltpu.VMEM((NJ, K, 128), F32),
            dma(2 * K), dma(2),
            dma(NJ), dma(NJ), dma(NJ), dma(NJ),
            dma(NI), dma(NI), dma(NI), dma(NI),
            dma(NI), dma(NI), dma(NJ), dma(NJ),
            dma(NI), dma(NI), dma(NJ), dma(NJ),
        ],
        compiler_params=pltpu.CompilerParams(
            collective_id=0, has_side_effects=True, vmem_limit_bytes=48 * 1024 * 1024
        ),
    )(tensor, b_init.T, c_init)
    return a, b.T, c


def solution(mesh):
    in_specs = (P(None, "ia", "ja"), P("ja", None), P())
    out_specs = (P(("ia", "ja"), None), P("ja", None), P())
    return jax.shard_map(body, mesh=mesh, in_specs=in_specs, out_specs=out_specs, check_vma=False)
```

time: 167 us -> 159 us (0.952)
  Pallas kernels: 163 us -> 155 us
    pallas_call x1, Pallas kernels: 163 us -> 155 us  [body(): pl.pallas_call(kernel, out_shape=(jax.ShapeDtypeStruct((R, R), F32), jax....]
    unnamed x5 -> x7, local copies, waits for them, and re-layouts: 2.92 us -> 3.45 us
where the time goes in v2:
time: 159 us
  Pallas kernels  155 us (97%)
  local copies, waits for them, and re-layouts  3.45 us (2%)
    pallas_call x1, Pallas kernels, body(): pl.pallas_call(kernel, out_shape=(jax.ShapeDtypeStruct((R, R), F32), jax....  155 us
    unnamed x7, local copies, waits for them, and re-layouts  3.45 us

profile of v2, /device:TPU:1, one launch (start us, length us, event | category | flops | bytes accessed | tf_op | source)
XLA Modules:
  0.0 158.9 jit_solution(5670640623674520358)
XLA Ops:
  0.6 0.0 copy-start
  0.6 0.9 copy-done
  1.5 0.0 copy-start.1
  1.5 0.7 copy-done.1
  2.2 154.8 %shard_map.58 = (f32[64,64]{1,0:T(8,128)S(1)}, f32[64,512]{1,0:T(8,128)S(1)}, f32[8,64]{1,0:T(8,128)S(1)}) custom-call(f32[8,1024,512]{2,1,0:T(8,128)} %t_hbm.1, f32[64,512]{1,0:T(8,128)S(1)} %bitcast.2, f32[8,64]{1,0:T(8,128)S(1)} %copy-done.1), custom_call_target="tpu_custom_call" | custom-call | tf_op jit(solution)/shard_map/pallas_call | solution.py:378
  157.0 0.6 copy.9
  157.7 0.7 copy.10
  158.3 0.6 copy.11
Async XLA Ops:
  0.6 0.9 copy-start
  1.5 0.7 copy-start.1

commit v3 on v2

--- a/solution.py
+++ b/solution.py
@@ -204,11 +204,13 @@
     for n in range(2 * K):
         k, rows = n // 2, slice(ROWS // 2 * (n % 2), ROWS // 2 * (n % 2 + 1))
         load(n).wait()
-        high, low = split(stage[k, rows])
-        t16[k, rows, :COLS] = high
-        t16[k, rows, COLS:] = low
-        prod[k, rows] = dot(t16[k, rows], w1[...], 1, 0)
-        if n == 10:
+        for half in range(2):
+            part = slice(rows.start + ROWS // 4 * half, rows.start + ROWS // 4 * (half + 1))
+            high, low = split(stage[k, part])
+            t16[k, part, :COLS] = high
+            t16[k, part, COLS:] = low
+            prod[k, part] = dot(high, w1[:COLS], 1, 0) + dot(low, w1[COLS:], 1, 0)
+        if n == 8:
             pl.semaphore_wait(barrier, NJ - 1 + NI - 1)
             share_gb.start_all()
 

time: 159 us -> 155 us (0.975)
  Pallas kernels: 155 us -> 151 us
    pallas_call x1, Pallas kernels: 155 us -> 151 us  [body(): pl.pallas_call(kernel, out_shape=(jax.ShapeDtypeStruct((R, R), F32), jax....]
where the time goes in v3:
time: 155 us
  Pallas kernels  151 us (97%)
  local copies, waits for them, and re-layouts  3.45 us (2%)
    pallas_call x1, Pallas kernels, body(): pl.pallas_call(kernel, out_shape=(jax.ShapeDtypeStruct((R, R), F32), jax....  151 us
    unnamed x7, local copies, waits for them, and re-layouts  3.45 us

profile of v3, /device:TPU:1, one launch (start us, length us, event | category | flops | bytes accessed | tf_op | source)
XLA Modules:
  0.0 155.1 jit_solution(6268957325922340174)
XLA Ops:
  0.6 0.0 copy-start
  0.6 0.9 copy-done
  1.5 0.0 copy-start.1
  1.5 0.7 copy-done.1
  2.2 151.0 %shard_map.58 = (f32[64,64]{1,0:T(8,128)S(1)}, f32[64,512]{1,0:T(8,128)S(1)}, f32[8,64]{1,0:T(8,128)S(1)}) custom-call(f32[8,1024,512]{2,1,0:T(8,128)} %t_hbm.1, f32[64,512]{1,0:T(8,128)S(1)} %bitcast.2, f32[8,64]{1,0:T(8,128)S(1)} %copy-done.1), custom_call_target="tpu_custom_call" | custom-call | tf_op jit(solution)/shard_map/pallas_call | solution.py:380
  153.3 0.6 copy.9
  153.9 0.7 copy.10
  154.5 0.6 copy.11
Async XLA Ops:
  0.6 0.9 copy-start
  1.5 0.7 copy-start.1

commit v4 on v3

--- a/solution.py
+++ b/solution.py
@@ -204,8 +204,8 @@
     for n in range(2 * K):
         k, rows = n // 2, slice(ROWS // 2 * (n % 2), ROWS // 2 * (n % 2 + 1))
         load(n).wait()
-        for half in range(2):
-            part = slice(rows.start + ROWS // 4 * half, rows.start + ROWS // 4 * (half + 1))
+        for piece in range(4):
+            part = slice(rows.start + ROWS // 8 * piece, rows.start + ROWS // 8 * (piece + 1))
             high, low = split(stage[k, part])
             t16[k, part, :COLS] = high
             t16[k, part, COLS:] = low

time: 155 us -> 155 us (level)
  no operation moved by 1% of the time
where the time goes in v4:
time: 155 us
  Pallas kernels  151 us (97%)
  local copies, waits for them, and re-layouts  3.45 us (2%)
    pallas_call x1, Pallas kernels, body(): pl.pallas_call(kernel, out_shape=(jax.ShapeDtypeStruct((R, R), F32), jax....  151 us
    unnamed x7, local copies, waits for them, and re-layouts  3.45 us

profile of v4, /device:TPU:1, one launch (start us, length us, event | category | flops | bytes accessed | tf_op | source)
XLA Modules:
  0.0 155.3 jit_solution(1936455795794596147)
XLA Ops:
  0.6 0.0 copy-start
  0.6 0.9 copy-done
  1.5 0.0 copy-start.1
  1.5 0.7 copy-done.1
  2.2 151.2 %shard_map.58 = (f32[64,64]{1,0:T(8,128)S(1)}, f32[64,512]{1,0:T(8,128)S(1)}, f32[8,64]{1,0:T(8,128)S(1)}) custom-call(f32[8,1024,512]{2,1,0:T(8,128)} %t_hbm.1, f32[64,512]{1,0:T(8,128)S(1)} %bitcast.2, f32[8,64]{1,0:T(8,128)S(1)} %copy-done.1), custom_call_target="tpu_custom_call" | custom-call | tf_op jit(solution)/shard_map/pallas_call | solution.py:380
  153.5 0.6 copy.9
  154.1 0.7 copy.10
  154.7 0.6 copy.11
Async XLA Ops:
  0.6 0.9 copy-start
  1.5 0.7 copy-start.1
